TPU v7x, 32 devices: a whole 2x2x4 slice. The times are simulated.
32 devices in a mesh: parts: 2 (over y), panel: 4 (over z), zone: 2 (over x), rhs: 2 (over core).
Axes of the slice: x: 2, y: 2, z: 4, core: 2. Of those that a mesh axis runs over, the one named last changes fastest.
Arguments:
- source: bfloat16 [4, 4096, 512], P(('parts', 'zone'), 'panel', 'rhs'), parts along dimension 0, may hold values from -6 to 6
- inverse: bfloat16 [4, 4096, 4096], P(('parts', 'zone'), 'panel'), parts along dimension 0, may hold values from -0.09375 to 0.09375
- coupling: bfloat16 [4, 4096, 4096], P(('parts', 'zone'), 'panel'), parts along dimension 0, may hold values from -0.078125 to 0.078125
Outputs:
- eliminated: bfloat16 [4, 4096, 512], P(('parts', 'zone'), 'panel', 'rhs'), parts along dimension 0
There are 2 independent parts, one for each index of `parts`. A program takes and returns all parts, laid end to end along the dimension named above; each array names one. Nothing has to cross between parts.
All inputs are finite; a program needn't handle non-finite values.
Results may differ from a plain program's by a relative error of at most 0.013.
Values may be sent and summed in bfloat16 or wider, within the bound.
A program may use at most 64 MiB of HBM per device.

v0:
```python
import jax
import jax.numpy as jnp
from jax import lax
from jax.sharding import PartitionSpec as P


def from_behind(block, axis, distance):
    devices = range(lax.axis_size(axis))
    route = [(i - distance, i) for i in devices if i - distance in devices]
    return lax.ppermute(block, axis, route)


def local(source, inverse, coupling):
    inverse_block = inverse[0]
    coupling_block = coupling[0]
    local_rhs = source[0]
    row_count = local_rhs.shape[0]
    local_cols = local_rhs.shape[1]
    batch_count = 4
    group_cols = local_cols // batch_count
    zone_count = lax.axis_size("zone")
    zone_index = lax.axis_index("zone")
    total_steps = zone_count + batch_count - 1
    reduced = jnp.dot(
        inverse_block,
        lax.all_gather(local_rhs, "panel", axis=0, tiled=True),
        preferred_element_type=jnp.float32,
    )

    def advance(position, carried):
        previous, result = carried
        micro_index = position - zone_index
        is_live = jnp.logical_and(micro_index >= 0, micro_index < batch_count)
        clipped = jnp.clip(micro_index, 0, batch_count - 1)
        start_col = clipped * group_cols
        incoming = from_behind(previous, "zone", 1)
        initial = lax.dynamic_slice_in_dim(reduced, start_col, group_cols, 1)
        combined = initial - jnp.dot(
            coupling_block,
            lax.all_gather(incoming, "panel", axis=0, tiled=True),
            preferred_element_type=jnp.float32,
        )
        rounded = combined.astype(jnp.bfloat16)
        current = lax.dynamic_slice_in_dim(result, start_col, group_cols, 1)
        updated = lax.dynamic_update_slice_in_dim(
            result, jnp.where(is_live, rounded, current), start_col, 1
        )
        return (rounded, updated)

    starting = (
        jnp.zeros((row_count, group_cols), jnp.bfloat16),
        jnp.zeros((row_count, local_cols), jnp.bfloat16),
    )
    _, result = lax.fori_loop(0, total_steps, advance, starting)
    return result[None]


def solution(mesh):
    in_specs = (
        P(("parts", "zone"), "panel", "rhs"),
        P(("parts", "zone"), "panel", None),
        P(("parts", "zone"), "panel", None),
    )
    out_specs = P(("parts", "zone"), "panel", "rhs")
    return jax.shard_map(local, mesh=mesh, in_specs=in_specs, out_specs=out_specs, check_vma=False)
```

profile of v0, /device:TPU:2, one launch (start us, length us, event | category | flops | bytes accessed | tf_op | source)
XLA Modules:
  0.0 211.0 jit_solution(5797174708042044751)
XLA Ops:
  6.5 0.0 all-gather.3.cloned.1.call-start
  6.5 0.7 all-gather.3.cloned.1.call-update
  7.3 48.9 %all-gather.3.cloned.1.call-done = bf16[1,4096,256]{2,1,0:T(8,128)(2,1)} async-done(((bf16[1,1024,256]{2,1,0:T(8,128)(2,1)}), bf16[1,4096,256]{2,1,0:T(8,128)(2,1)}) %all-gather.3.cloned.1.call-update) | async-done | bytes 2097168 | tf_op jit(solution)/shard_map/all_gather | solution.py:26
  56.1 6.3 %fusion.1 = f32[1024,256]{0,1:T(8,128)S(1)} fusion(bf16[1,1024,4096]{2,1,0:T(8,128)(2,1)} %param.6, bf16[1,4096,256]{2,1,0:T(8,128)(2,1)} %all-gather.3.cloned.1.call-done), kind=kOutput, calls=%fused_computation.4 | convolution fusion | flops 2147483648 | bytes 11534336 | tf_op jit(solution)/shard_map/dot_general | solution.py:24
  62.5 0.1 broadcast_in_dim.10
  62.5 140.6 %while.16 = (s32[]{:T(128)}, bf16[1024,64]{0,1:T(8,128)(2,1)S(1)}, bf16[1024,256]{0,1:T(8,128)(2,1)S(1)}, s32[]{:T(128)}, f32[1024,256]{0,1:T(8,128)S(1)}, /*ind...) while((s32[]{:T(128)}, bf16[1024,64]{0,1:T(8,128)(2,1)S(1)}, ...), condition=%wide.region_1.2_spmd.clone, body=%wide.region_0.1_spmd.clone.sunk | while | flops 537133056 | bytes 11010323 | solution.py:54
  62.6 1.3 collective-permute-start
  63.9 5.8 %collective-permute-done = bf16[1024,64]{0,1:T(8,128)(2,1)S(1)} collective-permute-done((bf16[1024,64]{0,1:T(8,128)(2,1)S(1)}, bf16[1024,64]{0,1:T(8,128)(2,1)S(1)}, u32[]{:S(2)}, u32[]{:S(2)}) %collective-permute-start) | collective-permute-done | bytes 131104 | tf_op jit(solution)/shard_map/while/body/eval_jaxpr/ppermute | solution.py:10
  69.7 16.1 %all_gather.13 = bf16[4096,64]{0,1:T(8,128)(2,1)S(1)} all-gather(bf16[1024,64]{0,1:T(8,128)(2,1)S(1)} %collective-permute-done), channel_id=1, replica_groups=mesh['parts'=2,'panel'=4,'zone'=2,'rhs'=2] {'panel'}, dimensions={0}, use_global_device_ids=true | all-gather | bytes 655360 | tf_op jit(solution)/shard_map/while/body/eval_jaxpr/all_gather | solution.py:40
  85.8 6.0 %select_dynamic-update-slice_fusion.2 = (bf16[1024,256]{0,1:T(8,128)(2,1)S(1)}, bf16[1024,64]{0,1:T(8,128)(2,1)S(1)}) fusion(bf16[1024,256]{0,1:T(8,128)(2,1)S(1)} %get-tuple-element.211, s32[]{:T(128)S(6)} %select_n.35, pred[]{:T(512)S(6)} %and.10, bf16[1024,4096]{1,0:T(8,128)(2,1)} %get-tuple-element.226, bf16[4096,64]{0,1:T(8,128)(2,1)S(1)} %all_gather.13, ...), kind=kOutput, calls=%fused_computation.2.clone.1 | convolution fusion | flops 537067520 | bytes 9568261 | tf_op jit(solution)/shard_map/while/body/eval_jaxpr/dot_general | solution.py:38
  91.9 1.3 collective-permute-start
  93.2 5.5 %collective-permute-done = bf16[1024,64]{0,1:T(8,128)(2,1)S(1)} collective-permute-done((bf16[1024,64]{0,1:T(8,128)(2,1)S(1)}, bf16[1024,64]{0,1:T(8,128)(2,1)S(1)}, u32[]{:S(2)}, u32[]{:S(2)}) %collective-permute-start) | collective-permute-done | bytes 131104 | tf_op jit(solution)/shard_map/while/body/eval_jaxpr/ppermute | solution.py:10
  98.7 15.5 %all_gather.13 = bf16[4096,64]{0,1:T(8,128)(2,1)S(1)} all-gather(bf16[1024,64]{0,1:T(8,128)(2,1)S(1)} %collective-permute-done), channel_id=1, replica_groups=mesh['parts'=2,'panel'=4,'zone'=2,'rhs'=2] {'panel'}, dimensions={0}, use_global_device_ids=true | all-gather | bytes 655360 | tf_op jit(solution)/shard_map/while/body/eval_jaxpr/all_gather | solution.py:40
  114.2 6.0 %select_dynamic-update-slice_fusion.2 = (bf16[1024,256]{0,1:T(8,128)(2,1)S(1)}, bf16[1024,64]{0,1:T(8,128)(2,1)S(1)}) fusion(bf16[1024,256]{0,1:T(8,128)(2,1)S(1)} %get-tuple-element.211, s32[]{:T(128)S(6)} %select_n.35, pred[]{:T(512)S(6)} %and.10, bf16[1024,4096]{1,0:T(8,128)(2,1)} %get-tuple-element.226, bf16[4096,64]{0,1:T(8,128)(2,1)S(1)} %all_gather.13, ...), kind=kOutput, calls=%fused_computation.2.clone.1 | convolution fusion | flops 537067520 | bytes 9568261 | tf_op jit(solution)/shard_map/while/body/eval_jaxpr/dot_general | solution.py:38
  120.3 1.3 collective-permute-start
  121.6 5.5 %collective-permute-done = bf16[1024,64]{0,1:T(8,128)(2,1)S(1)} collective-permute-done((bf16[1024,64]{0,1:T(8,128)(2,1)S(1)}, bf16[1024,64]{0,1:T(8,128)(2,1)S(1)}, u32[]{:S(2)}, u32[]{:S(2)}) %collective-permute-start) | collective-permute-done | bytes 131104 | tf_op jit(solution)/shard_map/while/body/eval_jaxpr/ppermute | solution.py:10
  127.1 14.7 %all_gather.13 = bf16[4096,64]{0,1:T(8,128)(2,1)S(1)} all-gather(bf16[1024,64]{0,1:T(8,128)(2,1)S(1)} %collective-permute-done), channel_id=1, replica_groups=mesh['parts'=2,'panel'=4,'zone'=2,'rhs'=2] {'panel'}, dimensions={0}, use_global_device_ids=true | all-gather | bytes 655360 | tf_op jit(solution)/shard_map/while/body/eval_jaxpr/all_gather | solution.py:40
  141.9 6.0 %select_dynamic-update-slice_fusion.2 = (bf16[1024,256]{0,1:T(8,128)(2,1)S(1)}, bf16[1024,64]{0,1:T(8,128)(2,1)S(1)}) fusion(bf16[1024,256]{0,1:T(8,128)(2,1)S(1)} %get-tuple-element.211, s32[]{:T(128)S(6)} %select_n.35, pred[]{:T(512)S(6)} %and.10, bf16[1024,4096]{1,0:T(8,128)(2,1)} %get-tuple-element.226, bf16[4096,64]{0,1:T(8,128)(2,1)S(1)} %all_gather.13, ...), kind=kOutput, calls=%fused_computation.2.clone.1 | convolution fusion | flops 537067520 | bytes 9568261 | tf_op jit(solution)/shard_map/while/body/eval_jaxpr/dot_general | solution.py:38
  148.0 1.3 collective-permute-start
  149.3 5.5 %collective-permute-done = bf16[1024,64]{0,1:T(8,128)(2,1)S(1)} collective-permute-done((bf16[1024,64]{0,1:T(8,128)(2,1)S(1)}, bf16[1024,64]{0,1:T(8,128)(2,1)S(1)}, u32[]{:S(2)}, u32[]{:S(2)}) %collective-permute-start) | collective-permute-done | bytes 131104 | tf_op jit(solution)/shard_map/while/body/eval_jaxpr/ppermute | solution.py:10
  154.8 14.7 %all_gather.13 = bf16[4096,64]{0,1:T(8,128)(2,1)S(1)} all-gather(bf16[1024,64]{0,1:T(8,128)(2,1)S(1)} %collective-permute-done), channel_id=1, replica_groups=mesh['parts'=2,'panel'=4,'zone'=2,'rhs'=2] {'panel'}, dimensions={0}, use_global_device_ids=true | all-gather | bytes 655360 | tf_op jit(solution)/shard_map/while/body/eval_jaxpr/all_gather | solution.py:40
  169.5 6.0 %select_dynamic-update-slice_fusion.2 = (bf16[1024,256]{0,1:T(8,128)(2,1)S(1)}, bf16[1024,64]{0,1:T(8,128)(2,1)S(1)}) fusion(bf16[1024,256]{0,1:T(8,128)(2,1)S(1)} %get-tuple-element.211, s32[]{:T(128)S(6)} %select_n.35, pred[]{:T(512)S(6)} %and.10, bf16[1024,4096]{1,0:T(8,128)(2,1)} %get-tuple-element.226, bf16[4096,64]{0,1:T(8,128)(2,1)S(1)} %all_gather.13, ...), kind=kOutput, calls=%fused_computation.2.clone.1 | convolution fusion | flops 537067520 | bytes 9568261 | tf_op jit(solution)/shard_map/while/body/eval_jaxpr/dot_general | solution.py:38
  175.6 1.3 collective-permute-start
  176.9 5.5 %collective-permute-done = bf16[1024,64]{0,1:T(8,128)(2,1)S(1)} collective-permute-done((bf16[1024,64]{0,1:T(8,128)(2,1)S(1)}, bf16[1024,64]{0,1:T(8,128)(2,1)S(1)}, u32[]{:S(2)}, u32[]{:S(2)}) %collective-permute-start) | collective-permute-done | bytes 131104 | tf_op jit(solution)/shard_map/while/body/eval_jaxpr/ppermute | solution.py:10
  182.4 14.7 %all_gather.13 = bf16[4096,64]{0,1:T(8,128)(2,1)S(1)} all-gather(bf16[1024,64]{0,1:T(8,128)(2,1)S(1)} %collective-permute-done), channel_id=1, replica_groups=mesh['parts'=2,'panel'=4,'zone'=2,'rhs'=2] {'panel'}, dimensions={0}, use_global_device_ids=true | all-gather | bytes 655360 | tf_op jit(solution)/shard_map/while/body/eval_jaxpr/all_gather | solution.py:40
  197.1 6.0 %select_dynamic-update-slice_fusion.2 = (bf16[1024,256]{0,1:T(8,128)(2,1)S(1)}, bf16[1024,64]{0,1:T(8,128)(2,1)S(1)}) fusion(bf16[1024,256]{0,1:T(8,128)(2,1)S(1)} %get-tuple-element.211, s32[]{:T(128)S(6)} %select_n.35, pred[]{:T(512)S(6)} %and.10, bf16[1024,4096]{1,0:T(8,128)(2,1)} %get-tuple-element.226, bf16[4096,64]{0,1:T(8,128)(2,1)S(1)} %all_gather.13, ...), kind=kOutput, calls=%fused_computation.2.clone.1 | convolution fusion | flops 537067520 | bytes 9568261 | tf_op jit(solution)/shard_map/while/body/eval_jaxpr/dot_general | solution.py:38
  203.1 1.0 copy.5
  (6 shorter events, 0.1 us)
Async XLA Ops:
  6.5 49.6 %all-gather.3.cloned.1.call-start = ((), (), s32[]{:S(2)}) async-start(), calls=%async_computation | async-start | bytes 2621440 | tf_op jit(solution)/shard_map/all_gather | solution.py:26
  62.6 7.1 %collective-permute-start = (bf16[1024,64]{0,1:T(8,128)(2,1)S(1)}, bf16[1024,64]{0,1:T(8,128)(2,1)S(1)}, u32[]{:S(2)}, u32[]{:S(2)}) collective-permute-start(bf16[1024,64]{0,1:T(8,128)(2,1)S(1)} %broadcast_select_fusion.2), channel_id=1, source_target_pairs={{0,2},{1,3},{4,6},{5,7},{8,10},{9,11},{12,14},{13,15},{16,18},{17,... | collective-permute-start | bytes 393224 | tf_op jit(solution)/shard_map/while/body/eval_jaxpr/ppermute | solution.py:10
  91.9 6.9 %collective-permute-start = (bf16[1024,64]{0,1:T(8,128)(2,1)S(1)}, bf16[1024,64]{0,1:T(8,128)(2,1)S(1)}, u32[]{:S(2)}, u32[]{:S(2)}) collective-permute-start(bf16[1024,64]{0,1:T(8,128)(2,1)S(1)} %broadcast_select_fusion.2), channel_id=1, source_target_pairs={{0,2},{1,3},{4,6},{5,7},{8,10},{9,11},{12,14},{13,15},{16,18},{17,... | collective-permute-start | bytes 393224 | tf_op jit(solution)/shard_map/while/body/eval_jaxpr/ppermute | solution.py:10
  120.3 6.9 %collective-permute-start = (bf16[1024,64]{0,1:T(8,128)(2,1)S(1)}, bf16[1024,64]{0,1:T(8,128)(2,1)S(1)}, u32[]{:S(2)}, u32[]{:S(2)}) collective-permute-start(bf16[1024,64]{0,1:T(8,128)(2,1)S(1)} %broadcast_select_fusion.2), channel_id=1, source_target_pairs={{0,2},{1,3},{4,6},{5,7},{8,10},{9,11},{12,14},{13,15},{16,18},{17,... | collective-permute-start | bytes 393224 | tf_op jit(solution)/shard_map/while/body/eval_jaxpr/ppermute | solution.py:10
  148.0 6.9 %collective-permute-start = (bf16[1024,64]{0,1:T(8,128)(2,1)S(1)}, bf16[1024,64]{0,1:T(8,128)(2,1)S(1)}, u32[]{:S(2)}, u32[]{:S(2)}) collective-permute-start(bf16[1024,64]{0,1:T(8,128)(2,1)S(1)} %broadcast_select_fusion.2), channel_id=1, source_target_pairs={{0,2},{1,3},{4,6},{5,7},{8,10},{9,11},{12,14},{13,15},{16,18},{17,... | collective-permute-start | bytes 393224 | tf_op jit(solution)/shard_map/while/body/eval_jaxpr/ppermute | solution.py:10
  175.6 6.9 %collective-permute-start = (bf16[1024,64]{0,1:T(8,128)(2,1)S(1)}, bf16[1024,64]{0,1:T(8,128)(2,1)S(1)}, u32[]{:S(2)}, u32[]{:S(2)}) collective-permute-start(bf16[1024,64]{0,1:T(8,128)(2,1)S(1)} %broadcast_select_fusion.2), channel_id=1, source_target_pairs={{0,2},{1,3},{4,6},{5,7},{8,10},{9,11},{12,14},{13,15},{16,18},{17,... | collective-permute-start | bytes 393224 | tf_op jit(solution)/shard_map/while/body/eval_jaxpr/ppermute | solution.py:10
Sparse Core Ops, SparseCore 0:
  8.9 47.1 all-gather.2
where the time goes:
time: 212 us; the launch traced here: 211 us
  waiting for transfers between devices  77.6 us (37%)
  blocking collectives  75.6 us (36%)
  matrix products  36.6 us (17%)
  between operations  13.4 us (6%)
  starting transfers between devices  6.46 us (3%)
    all_gather x5, blocking collectives, advance(): lax.all_gather(incoming, 'panel', axis=0, tiled=True)  75.6 us
    all_gather x1, waiting for transfers between devices, local(): lax.all_gather(local_rhs, 'panel', axis=0, tiled=True)  48.9 us
    dot_general x5, matrix products, advance(): jnp.dot(coupling_block, lax.all_gather(incoming, 'panel', axis=0, tiled=T...  30.2 us
    ppermute x5, waiting for transfers between devices, from_behind(): return lax.ppermute(block, axis, route)  28 us
    ppermute x5, starting transfers between devices, from_behind(): return lax.ppermute(block, axis, route)  6.46 us
    dot_general x1, matrix products, local(): jnp.dot(inverse_block, lax.all_gather(local_rhs, 'panel', axis=0, tiled=T...  6.35 us
  transfers between devices with their start and end apart: 6, of which 6 were waited for; matrix products, arithmetic and copies ran while one was open for 0% of the time, Pallas kernels for 0%

commit v1 on v0

v1 whole, which is shorter than its diff:
```python
import functools

import jax
import jax.numpy as jnp
from jax import lax
from jax.experimental import pallas as pl
from jax.experimental.pallas import tpu as pltpu
from jax.sharding import PartitionSpec as P

MESH = pl.DeviceIdType.MESH
RIGHT, LEFT = 0, 1
SOURCE_PIECES = 4
PIECES = 8
NEAR = 5


def kernel(
    panels, zones, source, inverse, coupling, out,
    inverse_v, coupling_v, rhs, previous, passing, total, mine,
    local_sem, rhs_send, rhs_recv, near_send, near_recv, far_send, far_recv, zone_send, zone_recv,
):
    panel, zone = lax.axis_index("panel"), lax.axis_index("zone")
    rows = mine.shape[0]
    tall, short = rows // SOURCE_PIECES, rows // PIECES
    tile = min(rows, 512)
    has_right, has_left = panel < panels - 1, panel > 0
    has_next, has_before = zone < zones - 1, zone > 0

    load_rhs = pltpu.make_async_copy(source.at[0], rhs.at[panel], local_sem.at[0])
    load_inverse = pltpu.make_async_copy(inverse.at[0], inverse_v, local_sem.at[1])
    load_coupling = pltpu.make_async_copy(coupling.at[0], coupling_v, local_sem.at[2])
    load_rhs.start()
    load_inverse.start()
    load_coupling.start()

    barrier = pltpu.get_barrier_semaphore()
    count = jnp.int32(0)
    for exists, axis, other in (
        (has_right, "panel", panel + 1),
        (has_left, "panel", panel - 1),
        (has_next, "zone", zone + 1),
        (has_before, "zone", zone - 1),
    ):
        @pl.when(exists)
        def _(axis=axis, other=other):
            pl.semaphore_signal(barrier, inc=1, device_id={axis: other}, device_id_type=MESH)

        count = count + exists.astype(jnp.int32)
    pl.semaphore_wait(barrier, count)

    def line(way, step, piece, from_ref, to_ref, send, recv):
        neighbour = panel + 1 if way == RIGHT else panel - 1
        return pltpu.make_async_remote_copy(
            src_ref=from_ref, dst_ref=to_ref,
            send_sem=send.at[way, step, piece], recv_sem=recv.at[way, step, piece],
            device_id={"panel": neighbour}, device_id_type=MESH,
        )

    def to_zone(block, piece, from_ref):
        return pltpu.make_async_remote_copy(
            src_ref=from_ref, dst_ref=previous.at[block, pl.ds(piece * short, short)],
            send_sem=zone_send.at[block, piece], recv_sem=zone_recv.at[block, piece],
            device_id={"zone": zone + 1}, device_id_type=MESH,
        )

    def ways(step):
        return (
            (RIGHT, panel - step, panel - step >= 0, has_right, has_left),
            (LEFT, panel + step, panel + step < panels, has_left, has_right),
        )

    def pass_on(step, pieces, own, place, send, recv, arrived=None):
        for piece in range(pieces):
            for way, block, exists, onward, _ in ways(step):
                @pl.when(exists)
                def _(piece=piece, way=way, block=block, onward=onward):
                    here = place(block, piece)
                    if step > 0:
                        line(way, step - 1, piece, here, here, send, recv).wait_recv()
                    if step < panels - 1:
                        @pl.when(onward)
                        def _():
                            start = own(piece) if step == 0 else here
                            line(way, step, piece, start, here, send, recv).start()
                    if step > 0 and arrived is not None:
                        arrived(block, piece)

    def sent(pieces, place, send, recv):
        for step in range(panels - 1):
            for piece in range(pieces):
                for way, block, exists, onward, _ in ways(step):
                    @pl.when(jnp.logical_and(exists, onward))
                    def _(step=step, piece=piece, way=way, block=block):
                        here = place(block, piece)
                        line(way, step, piece, here, here, send, recv).wait_send()

    def accumulate(matrix, block, vectors, kind):
        columns = pl.ds(pl.multiple_of(block * rows, rows), rows)

        @pl.loop(0, rows // tile)
        def _(i):
            part = pl.ds(pl.multiple_of(i * tile, tile), tile)
            product = jnp.dot(matrix[part, columns], vectors[block], preferred_element_type=jnp.float32)
            if kind == "set":
                total[part, :] = product
            elif kind == "add":
                total[part, :] += product
            else:
                total[part, :] -= product

    def rhs_place(block, piece):
        return rhs.at[block, pl.ds(piece * tall, tall)]

    for step in range(panels):
        pass_on(
            step, SOURCE_PIECES, lambda piece: source.at[0, pl.ds(piece * tall, tall)],
            rhs_place, rhs_send, rhs_recv,
        )
        if step == 0:
            load_rhs.wait()
            load_inverse.wait()
            accumulate(inverse_v, panel, rhs, "set")
        else:
            for _, block, exists, _, _ in ways(step):
                @pl.when(exists)
                def _(block=block):
                    accumulate(inverse_v, block, rhs, "add")
    load_coupling.wait()

    def near_place(block, piece):
        return previous.at[block, pl.ds(piece * short, short)]

    def far_arrived(block):
        for piece in range(NEAR, PIECES):
            to_zone(block, piece, near_place(block, piece)).wait_recv()

    @pl.when(has_before)
    def _():
        for step in range(panels):
            if step == 0:
                for piece in range(NEAR):
                    to_zone(panel, piece, near_place(panel, piece)).wait_recv()
                    for way, _, _, onward, _ in ways(0):
                        @pl.when(onward)
                        def _(way=way, piece=piece):
                            here = near_place(panel, piece)
                            line(way, 0, piece, here, here, near_send, near_recv).start()
                far_arrived(panel)
                accumulate(coupling_v, panel, previous, "subtract")
            else:
                pass_on(step, NEAR, None, near_place, near_send, near_recv)
                for _, block, exists, _, _ in ways(step):
                    @pl.when(exists)
                    def _(block=block):
                        far_arrived(block)
                        accumulate(coupling_v, block, previous, "subtract")

    mine[...] = total[...].astype(mine.dtype)
    store = pltpu.make_async_copy(mine, out.at[0], local_sem.at[3])
    store.start()

    def own(piece):
        return mine.at[pl.ds(piece * short, short)]

    def far_place(block, piece):
        return passing.at[block, pl.ds(piece * short, short)]

    def hand_over(block, piece):
        to_zone(block, NEAR + piece, far_place(block, piece)).start()

    @pl.when(has_next)
    def _():
        for piece in range(NEAR):
            to_zone(panel, piece, own(piece)).start()
        for step in range(panels):
            pass_on(
                step, PIECES - NEAR, lambda piece: own(NEAR + piece), far_place, far_send, far_recv, hand_over
            )
            if step == 0:
                for piece in range(NEAR, PIECES):
                    to_zone(panel, piece, own(piece)).start()

    sent(SOURCE_PIECES, rhs_place, rhs_send, rhs_recv)

    @pl.when(has_before)
    def _():
        sent(NEAR, near_place, near_send, near_recv)

    @pl.when(has_next)
    def _():
        sent(PIECES - NEAR, far_place, far_send, far_recv)
        for piece in range(NEAR):
            to_zone(panel, piece, own(piece)).wait_send()
        for block in range(panels):
            for piece in range(NEAR, PIECES):
                to_zone(block, piece, own(piece)).wait_send()
    store.wait()


def solution(mesh):
    panels, zones = mesh.shape["panel"], mesh.shape["zone"]

    def local(source, inverse, coupling):
        _, rows, cols = source.shape
        unknowns = inverse.shape[2]
        far = PIECES - NEAR
        steps = max(panels - 1, 1)
        dma = pltpu.SemaphoreType.DMA
        anywhere = pl.BlockSpec(memory_space=pl.ANY)
        return pl.pallas_call(
            functools.partial(kernel, panels, zones),
            out_shape=jax.ShapeDtypeStruct(source.shape, jnp.bfloat16),
            in_specs=[anywhere] * 3,
            out_specs=anywhere,
            scratch_shapes=[
                pltpu.VMEM((rows, unknowns), jnp.bfloat16),
                pltpu.VMEM((rows, unknowns), jnp.bfloat16),
                pltpu.VMEM((panels, rows, cols), jnp.bfloat16),
                pltpu.VMEM((panels, rows, cols), jnp.bfloat16),
                pltpu.VMEM((panels, rows // PIECES * far, cols), jnp.bfloat16),
                pltpu.VMEM((rows, cols), jnp.float32),
                pltpu.VMEM((rows, cols), jnp.bfloat16),
                dma((4,)),
                dma((2, steps, SOURCE_PIECES)), dma((2, steps, SOURCE_PIECES)),
                dma((2, steps, NEAR)), dma((2, steps, NEAR)),
                dma((2, steps, far)), dma((2, steps, far)),
                dma((panels, PIECES)), dma((panels, PIECES)),
            ],
            compiler_params=pltpu.CompilerParams(
                collective_id=0, has_side_effects=True, vmem_limit_bytes=48 * 2**20
            ),
            cost_estimate=pl.CostEstimate(
                flops=4 * rows * unknowns * cols, bytes_accessed=4 * rows * unknowns, transcendentals=0
            ),
        )(source, inverse, coupling)

    return jax.shard_map(
        local,
        mesh=mesh,
        in_specs=(
            P(("parts", "zone"), "panel", "rhs"),
            P(("parts", "zone"), "panel", None),
            P(("parts", "zone"), "panel", None),
        ),
        out_specs=P(("parts", "zone"), "panel", "rhs"),
        check_vma=False,
    )
```

time: 212 us -> 67.5 us (0.32)
  waiting for transfers between devices: 77.6 us -> 0 us
  blocking collectives: 75.6 us -> 0 us
  Pallas kernels: 0 us -> 65.5 us
  matrix products: 36.6 us -> 0 us
  between operations: 13.4 us -> 0.01 us
  starting transfers between devices: 6.46 us -> 0 us
    all_gather x5 -> x0, blocking collectives: 75.6 us -> none  [advance(): lax.all_gather(incoming, 'panel', axis=0, tiled=True)]
    pallas_call x0 -> x1, Pallas kernels: none -> 65.5 us  [local(): pl.pallas_call(functools.partial(kernel, panels, zones), out_shape=jax.Sh...]
    all_gather x1 -> x0, waiting for transfers between devices: 48.9 us -> none  [local(): lax.all_gather(local_rhs, 'panel', axis=0, tiled=True)]
    dot_general x6 -> x0, matrix products: 36.6 us -> none  [the longest x5 30.2 us: advance(): jnp.dot(coupling_block, lax.all_gather(incoming, 'panel', axis=0, tiled=T...]
    ppermute x5 -> x0, waiting for transfers between devices: 28 us -> none  [from_behind(): return lax.ppermute(block, axis, route)]
    ppermute x5 -> x0, starting transfers between devices: 6.46 us -> none  [from_behind(): return lax.ppermute(block, axis, route)]
  transfers between devices with their start and end apart: 6 -> 0, of which waited for: 6 -> 0; matrix products, arithmetic and copies ran while one was open for 0% -> 0% of each run, Pallas kernels for 0% -> 0%
where the time goes in v1:
time: 67.5 us; the launch traced here: 67.4 us
  Pallas kernels  65.5 us (97%)
  local copies, waits for them, and re-layouts  1.84 us (3%)
    pallas_call x1, Pallas kernels, local(): pl.pallas_call(functools.partial(kernel, panels, zones), out_shape=jax.Sh...  65.5 us
    unnamed x3, local copies, waits for them, and re-layouts  1.84 us

profile of v1, /device:TPU:2, one launch (start us, length us, event | category | flops | bytes accessed | tf_op | source)
XLA Modules:
  0.0 67.4 jit_solution(8023545043274312064)
XLA Ops:
  0.0 0.0 copy-start
  0.0 1.0 %copy-done = bf16[1,1024,256]{2,1,0:T(8,128)(2,1)S(1)} copy-done((bf16[1,1024,256]{2,1,0:T(8,128)(2,1)S(1)}, bf16[1,1024,256]{2,1,0:T(8,128)(2,1)}, u32[]{:S(2)}) %copy-start) | copy-done | bytes 524312
  1.0 65.5 %shard_map.37 = bf16[1,1024,256]{2,1,0:T(8,128)(2,1)S(1)} custom-call(bf16[1,1024,256]{2,1,0:T(8,128)(2,1)S(1)} %copy-done, bf16[1,1024,4096]{2,1,0:T(8,128)(2,1)} %inverse.1, bf16[1,1024,4096]{2,1,0:T(8,128)(2,1)} %coupling.1), custom_call_target="tpu_custom_call" | custom-call | flops 4294967296 | bytes 16777216 | tf_op jit(solution)/shard_map/pallas_call | solution.py:210
  66.6 0.8 %copy.5 = bf16[1,1024,256]{2,1,0:T(8,128)(2,1)} copy(bf16[1,1024,256]{2,1,0:T(8,128)(2,1)S(1)} %shard_map.37) | data formatting | bytes 1048576
Async XLA Ops:
  0.0 1.0 %copy-start = (bf16[1,1024,256]{2,1,0:T(8,128)(2,1)S(1)}, bf16[1,1024,256]{2,1,0:T(8,128)(2,1)}, u32[]{:S(2)}) copy-start(bf16[1,1024,256]{2,1,0:T(8,128)(2,1)} %source.1) | copy-start | bytes 1572868

commit v2 on v1

v2 whole, which is shorter than its diff:
```python
import functools

import jax
import jax.numpy as jnp
from jax import lax
from jax.experimental import pallas as pl
from jax.experimental.pallas import tpu as pltpu
from jax.sharding import PartitionSpec as P

MESH = pl.DeviceIdType.MESH
RIGHT, LEFT = 0, 1
CHUNKS = 2
SOURCE_PIECES = 4
PIECES = 8
NEAR = (8, 2)
FAR = max(PIECES - near for near in NEAR)


def kernel(
    panels, zones, source, inverse, coupling, out,
    inverse_v, coupling_v, rhs, previous, passing, total, mine,
    local_sem, rhs_send, rhs_recv, near_send, near_recv, far_send, far_recv, zone_send, zone_recv,
):
    panel, zone = lax.axis_index("panel"), lax.axis_index("zone")
    _, rows, width = mine.shape
    tall, short = rows // SOURCE_PIECES, rows // PIECES
    tile = min(rows, 512)
    has_right, has_left = panel < panels - 1, panel > 0
    has_next, has_before = zone < zones - 1, zone > 0

    def columns_of(chunk):
        return pl.ds(chunk * width, width)

    load_rhs = [
        pltpu.make_async_copy(source.at[0, :, columns_of(c)], rhs.at[c, panel], local_sem.at[c])
        for c in range(CHUNKS)
    ]
    load_inverse = pltpu.make_async_copy(inverse.at[0], inverse_v, local_sem.at[CHUNKS])
    load_coupling = pltpu.make_async_copy(coupling.at[0], coupling_v, local_sem.at[CHUNKS + 1])
    for load in load_rhs:
        load.start()

    barrier = pltpu.get_barrier_semaphore()
    count = jnp.int32(0)
    for exists, axis, other in (
        (has_right, "panel", panel + 1),
        (has_left, "panel", panel - 1),
        (has_next, "zone", zone + 1),
        (has_before, "zone", zone - 1),
    ):
        @pl.when(exists)
        def _(axis=axis, other=other):
            pl.semaphore_signal(barrier, inc=1, device_id={axis: other}, device_id_type=MESH)

        count = count + exists.astype(jnp.int32)
    for load in load_rhs:
        load.wait()
    load_inverse.start()
    load_coupling.start()
    pl.semaphore_wait(barrier, count)

    def line(way, chunk, step, piece, here, send, recv, start=None):
        neighbour = panel + 1 if way == RIGHT else panel - 1
        return pltpu.make_async_remote_copy(
            src_ref=here if start is None else start, dst_ref=here,
            send_sem=send.at[chunk, way, step, piece], recv_sem=recv.at[chunk, way, step, piece],
            device_id={"panel": neighbour}, device_id_type=MESH,
        )

    def to_zone(chunk, block, piece, from_ref):
        return pltpu.make_async_remote_copy(
            src_ref=from_ref, dst_ref=previous.at[chunk, block, pl.ds(piece * short, short)],
            send_sem=zone_send.at[chunk, block, piece], recv_sem=zone_recv.at[chunk, block, piece],
            device_id={"zone": zone + 1}, device_id_type=MESH,
        )

    def ways(step):
        return (
            (RIGHT, panel - step, panel - step >= 0, has_right),
            (LEFT, panel + step, panel + step < panels, has_left),
        )

    def pass_on(chunk, step, pieces, place, send, recv, own=None, after=None):
        for piece in range(pieces):
            for way, block, exists, onward in ways(step):
                @pl.when(exists)
                def _(piece=piece, way=way, block=block, onward=onward):
                    here = place(chunk, block, piece)
                    if step > 0:
                        line(way, chunk, step - 1, piece, here, send, recv).wait_recv()
                    if step < panels - 1:
                        @pl.when(onward)
                        def _():
                            start = own(piece) if own is not None else None
                            line(way, chunk, step, piece, here, send, recv, start).start()
                    if step > 0 and after is not None:
                        after(block, piece)
            if step == 0 and after is not None:
                after(panel, piece)

    def sent(chunk, pieces, place, send, recv):
        for step in range(panels - 1):
            for piece in range(pieces):
                for way, block, exists, onward in ways(step):
                    @pl.when(jnp.logical_and(exists, onward))
                    def _(step=step, piece=piece, way=way, block=block):
                        line(way, chunk, step, piece, place(chunk, block, piece), send, recv).wait_send()

    def accumulate(matrix, chunk, block, vectors, kind):
        columns = pl.ds(pl.multiple_of(block * rows, rows), rows)

        @pl.loop(0, rows // tile)
        def _(i):
            part = pl.ds(pl.multiple_of(i * tile, tile), tile)
            product = jnp.dot(matrix[part, columns], vectors[chunk, block], preferred_element_type=jnp.float32)
            if kind == "set":
                total[chunk, part, :] = product
            elif kind == "add":
                total[chunk, part, :] += product
            else:
                total[chunk, part, :] -= product

    def rhs_place(chunk, block, piece):
        return rhs.at[chunk, block, pl.ds(piece * tall, tall)]

    def rhs_pass(chunk, step):
        pass_on(chunk, step, SOURCE_PIECES, rhs_place, rhs_send, rhs_recv)

    def rhs_product(chunk, step):
        if step == 0:
            accumulate(inverse_v, chunk, panel, rhs, "set")
        else:
            for _, block, exists, _ in ways(step):
                @pl.when(exists)
                def _(block=block):
                    accumulate(inverse_v, chunk, block, rhs, "add")

    def near_place(chunk, block, piece):
        return previous.at[chunk, block, pl.ds(piece * short, short)]

    def previous_pass(chunk, step):
        if step == 0:
            for piece in range(NEAR[chunk]):
                here = near_place(chunk, panel, piece)
                to_zone(chunk, panel, piece, here).wait_recv()
                if panels > 1:
                    for way, _, _, onward in ways(0):
                        @pl.when(onward)
                        def _(way=way, piece=piece, here=here):
                            line(way, chunk, 0, piece, here, near_send, near_recv).start()
        else:
            pass_on(chunk, step, NEAR[chunk], near_place, near_send, near_recv)

    def previous_product(chunk, step):
        def one(block):
            for piece in range(NEAR[chunk], PIECES):
                to_zone(chunk, block, piece, near_place(chunk, block, piece)).wait_recv()
            accumulate(coupling_v, chunk, block, previous, "subtract")

        if step == 0:
            one(panel)
        else:
            for _, block, exists, _ in ways(step):
                @pl.when(exists)
                def _(block=block):
                    one(block)

    def own(chunk, piece):
        return mine.at[chunk, pl.ds(piece * short, short)]

    def far_place(chunk, block, piece):
        return passing.at[block, pl.ds(piece * short, short)]

    def finish(chunk):
        result = total[chunk].astype(mine.dtype)
        out[0, :, columns_of(chunk)] = result

        @pl.when(has_next)
        def _():
            mine[chunk] = result
            near = NEAR[chunk]
            for piece in range(near):
                to_zone(chunk, panel, piece, own(chunk, piece)).start()

            def hand_over(block, piece):
                from_ref = own(chunk, near + piece) if step == 0 else far_place(chunk, block, piece)
                to_zone(chunk, block, near + piece, from_ref).start()

            if near < PIECES:
                for step in range(panels):
                    pass_on(
                        chunk, step, PIECES - near, far_place, far_send, far_recv,
                        (lambda piece: own(chunk, near + piece)) if step == 0 else None, hand_over,
                    )

    rhs_pass(0, 0)
    load_inverse.wait()
    rhs_product(0, 0)
    for step in range(1, panels):
        if step == panels - 1:
            rhs_pass(1, 0)
        rhs_pass(0, step)
        rhs_product(0, step)
    if panels == 1:
        rhs_pass(1, 0)

    @pl.when(jnp.logical_not(has_before))
    def _():
        finish(0)

    load_coupling.wait()
    for step in range(panels):
        if step > 0:
            rhs_pass(1, step)

        @pl.when(has_before)
        def _(step=step):
            previous_pass(0, step)

        rhs_product(1, step)

        @pl.when(has_before)
        def _(step=step):
            previous_product(0, step)

    @pl.when(has_before)
    def _():
        finish(0)
        for step in range(panels):
            previous_pass(1, step)
            previous_product(1, step)

    finish(1)

    for chunk in range(CHUNKS):
        sent(chunk, SOURCE_PIECES, rhs_place, rhs_send, rhs_recv)

        @pl.when(has_before)
        def _(chunk=chunk):
            sent(chunk, NEAR[chunk], near_place, near_send, near_recv)

        @pl.when(has_next)
        def _(chunk=chunk):
            sent(chunk, PIECES - NEAR[chunk], far_place, far_send, far_recv)
            for piece in range(NEAR[chunk]):
                to_zone(chunk, panel, piece, own(chunk, piece)).wait_send()
            for block in range(panels):
                for piece in range(NEAR[chunk], PIECES):
                    to_zone(chunk, block, piece, own(chunk, piece)).wait_send()


def solution(mesh):
    panels, zones = mesh.shape["panel"], mesh.shape["zone"]

    def local(source, inverse, coupling):
        _, rows, cols = source.shape
        unknowns = inverse.shape[2]
        width = cols // CHUNKS
        steps = max(panels - 1, 1)
        dma = pltpu.SemaphoreType.DMA
        anywhere = pl.BlockSpec(memory_space=pltpu.HBM)
        return pl.pallas_call(
            functools.partial(kernel, panels, zones),
            out_shape=jax.ShapeDtypeStruct(source.shape, jnp.bfloat16),
            in_specs=[anywhere] * 3,
            out_specs=pl.BlockSpec(memory_space=pltpu.VMEM),
            scratch_shapes=[
                pltpu.VMEM((rows, unknowns), jnp.bfloat16),
                pltpu.VMEM((rows, unknowns), jnp.bfloat16),
                pltpu.VMEM((CHUNKS, panels, rows, width), jnp.bfloat16),
                pltpu.VMEM((CHUNKS, panels, rows, width), jnp.bfloat16),
                pltpu.VMEM((panels, rows // PIECES * FAR, width), jnp.bfloat16),
                pltpu.VMEM((CHUNKS, rows, width), jnp.float32),
                pltpu.VMEM((CHUNKS, rows, width), jnp.bfloat16),
                dma((CHUNKS + 2,)),
                dma((CHUNKS, 2, steps, SOURCE_PIECES)), dma((CHUNKS, 2, steps, SOURCE_PIECES)),
                dma((CHUNKS, 2, steps, PIECES)), dma((CHUNKS, 2, steps, PIECES)),
                dma((CHUNKS, 2, steps, FAR)), dma((CHUNKS, 2, steps, FAR)),
                dma((CHUNKS, panels, PIECES)), dma((CHUNKS, panels, PIECES)),
            ],
            compiler_params=pltpu.CompilerParams(
                collective_id=0, has_side_effects=True, vmem_limit_bytes=64 * 2**20 - 2**18
            ),
            cost_estimate=pl.CostEstimate(
                flops=4 * rows * unknowns * cols, bytes_accessed=4 * rows * unknowns, transcendentals=0
            ),
        )(source, inverse, coupling)

    return jax.shard_map(
        local,
        mesh=mesh,
        in_specs=(
            P(("parts", "zone"), "panel", "rhs"),
            P(("parts", "zone"), "panel", None),
            P(("parts", "zone"), "panel", None),
        ),
        out_specs=P(("parts", "zone"), "panel", "rhs"),
        check_vma=False,
    )
```

time: 67.5 us -> 75.7 us (1.12)
  Pallas kernels: 65.5 us -> 73.6 us
    pallas_call x1, Pallas kernels: 65.5 us -> 73.6 us  [local(): pl.pallas_call(functools.partial(kernel, panels, zones), out_shape=jax.Sh...]
    unnamed x3 -> x1, local copies, waits for them, and re-layouts: 1.84 us -> 1.87 us
where the time goes in v2:
time: 75.7 us; the launch traced here: 75.5 us
  Pallas kernels  73.6 us (97%)
  local copies, waits for them, and re-layouts  1.87 us (2%)
    pallas_call x1, Pallas kernels, local(): pl.pallas_call(functools.partial(kernel, panels, zones), out_shape=jax.Sh...  73.6 us
    unnamed x1, local copies, waits for them, and re-layouts  1.87 us

profile of v2, /device:TPU:2, one launch (start us, length us, event | category | flops | bytes accessed | tf_op | source)
XLA Modules:
  0.0 75.5 jit_solution(918943983008867612)
XLA Ops:
  0.0 73.6 %shard_map.37 = bf16[1,1024,256]{2,1,0:T(8,128)(2,1)} custom-call(bf16[1,1024,256]{2,1,0:T(8,128)(2,1)} %source.1, bf16[1,1024,4096]{2,1,0:T(8,128)(2,1)} %inverse.1, bf16[1,1024,4096]{2,1,0:T(8,128)(2,1)} %coupling.1), custom_call_target="tpu_custom_call" | custom-call | flops 4294967296 | bytes 16777216 | tf_op jit(solution)/shard_map/pallas_call | solution.py:262
  73.6 1.9 %copy.5 = bf16[1,1024,256]{2,1,0:T(8,128)(2,1)} copy(bf16[1,1024,256]{2,1,0:T(8,128)(2,1)} %shard_map.37) | data formatting | bytes 1048576

commit v3 on v2

--- a/solution.py
+++ b/solution.py
@@ -106,19 +106,22 @@
                     def _(step=step, piece=piece, way=way, block=block):
                         line(way, chunk, step, piece, place(chunk, block, piece), send, recv).wait_send()
 
-    def accumulate(matrix, chunk, block, vectors, kind):
+    def accumulate(matrix, chunks, block, vectors, kind):
         columns = pl.ds(pl.multiple_of(block * rows, rows), rows)
 
         @pl.loop(0, rows // tile)
         def _(i):
             part = pl.ds(pl.multiple_of(i * tile, tile), tile)
-            product = jnp.dot(matrix[part, columns], vectors[chunk, block], preferred_element_type=jnp.float32)
-            if kind == "set":
-                total[chunk, part, :] = product
-            elif kind == "add":
-                total[chunk, part, :] += product
-            else:
-                total[chunk, part, :] -= product
+            wide = jnp.concatenate([vectors[c, block] for c in chunks], axis=1)
+            product = jnp.dot(matrix[part, columns], wide, preferred_element_type=jnp.float32)
+            for n, c in enumerate(chunks):
+                one = product[:, n * width:(n + 1) * width]
+                if kind == "set":
+                    total[c, part, :] = one
+                elif kind == "add":
+                    total[c, part, :] += one
+                else:
+                    total[c, part, :] -= one
 
     def rhs_place(chunk, block, piece):
         return rhs.at[chunk, block, pl.ds(piece * tall, tall)]
@@ -126,14 +129,14 @@
     def rhs_pass(chunk, step):
         pass_on(chunk, step, SOURCE_PIECES, rhs_place, rhs_send, rhs_recv)
 
-    def rhs_product(chunk, step):
+    def rhs_product(chunks, step):
         if step == 0:
-            accumulate(inverse_v, chunk, panel, rhs, "set")
+            accumulate(inverse_v, chunks, panel, rhs, "set")
         else:
             for _, block, exists, _ in ways(step):
                 @pl.when(exists)
                 def _(block=block):
-                    accumulate(inverse_v, chunk, block, rhs, "add")
+                    accumulate(inverse_v, chunks, block, rhs, "add")
 
     def near_place(chunk, block, piece):
         return previous.at[chunk, block, pl.ds(piece * short, short)]
@@ -151,11 +154,12 @@
         else:
             pass_on(chunk, step, NEAR[chunk], near_place, near_send, near_recv)
 
-    def previous_product(chunk, step):
+    def previous_product(step):
         def one(block):
-            for piece in range(NEAR[chunk], PIECES):
-                to_zone(chunk, block, piece, near_place(chunk, block, piece)).wait_recv()
-            accumulate(coupling_v, chunk, block, previous, "subtract")
+            for chunk in range(CHUNKS):
+                for piece in range(NEAR[chunk], PIECES):
+                    to_zone(chunk, block, piece, near_place(chunk, block, piece)).wait_recv()
+            accumulate(coupling_v, (0, 1), block, previous, "subtract")
 
         if step == 0:
             one(panel)
@@ -193,42 +197,84 @@
                         (lambda piece: own(chunk, near + piece)) if step == 0 else None, hand_over,
                     )
 
+    last = panels - 1
+    is_first = jnp.logical_not(has_before)
+
+    def in_first(action):
+        pl.when(is_first)(action)
+
+    def in_later(action):
+        pl.when(has_before)(action)
+
     rhs_pass(0, 0)
-    load_inverse.wait()
-    rhs_product(0, 0)
     for step in range(1, panels):
-        if step == panels - 1:
+        rhs_pass(0, step)
+        if step == 1:
             rhs_pass(1, 0)
-        rhs_pass(0, step)
-        rhs_product(0, step)
+            load_inverse.wait()
+        if step == last:
+            @in_first
+            def _(step=step):
+                rhs_product((0,), step - 1)
+                rhs_product((0,), step)
+                finish(0)
+        if step > 1:
+            rhs_pass(1, step - 1)
+
+        @in_first
+        def _(step=step):
+            if step < last:
+                rhs_product((0,), step - 1)
+            rhs_product((1,), step - 1)
+
+        if step == last:
+            @in_later
+            def _():
+                previous_pass(0, 0)
+
+        @in_later
+        def _(step=step):
+            rhs_product((0, 1), step - 1)
+
     if panels == 1:
         rhs_pass(1, 0)
-
-    @pl.when(jnp.logical_not(has_before))
+        load_inverse.wait()
+
+        @in_first
+        def _():
+            rhs_product((0,), 0)
+            finish(0)
+
+        @in_later
+        def _():
+            previous_pass(0, 0)
+    else:
+        rhs_pass(1, last)
+
+    @in_first
     def _():
+        rhs_product((1,), last)
+        load_coupling.wait()
+
+    @in_later
+    def _():
+        if last >= 1:
+            previous_pass(0, 1)
+        rhs_product((0, 1), last)
+        load_coupling.wait()
+        previous_pass(1, 0)
+        for step in range(2, panels):
+            previous_pass(0, step)
+            previous_pass(1, step - 1)
+            if step == 2:
+                previous_product(0)
+            previous_product(step - 1)
+        if last <= 1:
+            previous_product(0)
+        if last >= 1:
+            previous_pass(1, last)
+            previous_product(last)
         finish(0)
-
-    load_coupling.wait()
-    for step in range(panels):
-        if step > 0:
-            rhs_pass(1, step)
-
-        @pl.when(has_before)
-        def _(step=step):
-            previous_pass(0, step)
-
-        rhs_product(1, step)
-
-        @pl.when(has_before)
-        def _(step=step):
-            previous_product(0, step)
-
-    @pl.when(has_before)
-    def _():
-        finish(0)
-        for step in range(panels):
-            previous_pass(1, step)
-            previous_product(1, step)
 
     finish(1)
 
@@ -279,7 +325,7 @@
                 dma((CHUNKS, panels, PIECES)), dma((CHUNKS, panels, PIECES)),
             ],
             compiler_params=pltpu.CompilerParams(
-                collective_id=0, has_side_effects=True, vmem_limit_bytes=64 * 2**20 - 2**18
+                collective_id=0, has_side_effects=True, vmem_limit_bytes=48 * 2**20
             ),
             cost_estimate=pl.CostEstimate(
                 flops=4 * rows * unknowns * cols, bytes_accessed=4 * rows * unknowns, transcendentals=0

time: 75.7 us -> 67 us (0.89)
  Pallas kernels: 73.6 us -> 65 us
    pallas_call x1, Pallas kernels: 73.6 us -> 65 us  [local(): pl.pallas_call(functools.partial(kernel, panels, zones), out_shape=jax.Sh...]
    unnamed x1 -> x3, local copies, waits for them, and re-layouts: 1.87 us -> 1.84 us
where the time goes in v3:
time: 67 us; the launch traced here: 66.8 us
  Pallas kernels  65 us (97%)
  local copies, waits for them, and re-layouts  1.84 us (3%)
    pallas_call x1, Pallas kernels, local(): pl.pallas_call(functools.partial(kernel, panels, zones), out_shape=jax.Sh...  65 us
    unnamed x3, local copies, waits for them, and re-layouts  1.84 us

profile of v3, /device:TPU:2, one launch (start us, length us, event | category | flops | bytes accessed | tf_op | source)
XLA Modules:
  0.0 66.8 jit_solution(12757859419182030728)
XLA Ops:
  0.0 0.0 copy-start
  0.0 1.0 %copy-done = bf16[1,1024,256]{2,1,0:T(8,128)(2,1)S(1)} copy-done((bf16[1,1024,256]{2,1,0:T(8,128)(2,1)S(1)}, bf16[1,1024,256]{2,1,0:T(8,128)(2,1)}, u32[]{:S(2)}) %copy-start) | copy-done | bytes 524312
  1.0 65.0 %shard_map.37 = bf16[1,1024,256]{2,1,0:T(8,128)(2,1)S(1)} custom-call(bf16[1,1024,256]{2,1,0:T(8,128)(2,1)S(1)} %copy-done, bf16[1,1024,4096]{2,1,0:T(8,128)(2,1)} %inverse.1, bf16[1,1024,4096]{2,1,0:T(8,128)(2,1)} %coupling.1), custom_call_target="tpu_custom_call" | custom-call | flops 4294967296 | bytes 16777216 | tf_op jit(solution)/shard_map/pallas_call | solution.py:308
  66.0 0.8 %copy.5 = bf16[1,1024,256]{2,1,0:T(8,128)(2,1)} copy(bf16[1,1024,256]{2,1,0:T(8,128)(2,1)S(1)} %shard_map.37) | data formatting | bytes 1048576
Async XLA Ops:
  0.0 1.0 %copy-start = (bf16[1,1024,256]{2,1,0:T(8,128)(2,1)S(1)}, bf16[1,1024,256]{2,1,0:T(8,128)(2,1)}, u32[]{:S(2)}) copy-start(bf16[1,1024,256]{2,1,0:T(8,128)(2,1)} %source.1) | copy-start | bytes 1572868

commit v4 on v3

--- a/solution.py
+++ b/solution.py
@@ -81,7 +81,7 @@
         )
 
     def pass_on(chunk, step, pieces, place, send, recv, own=None, after=None):
-        for piece in range(pieces):
+        for piece in pieces:
             for way, block, exists, onward in ways(step):
                 @pl.when(exists)
                 def _(piece=piece, way=way, block=block, onward=onward):
@@ -95,8 +95,6 @@
                             line(way, chunk, step, piece, here, send, recv, start).start()
                     if step > 0 and after is not None:
                         after(block, piece)
-            if step == 0 and after is not None:
-                after(panel, piece)
 
     def sent(chunk, pieces, place, send, recv):
         for step in range(panels - 1):
@@ -106,13 +104,15 @@
                     def _(step=step, piece=piece, way=way, block=block):
                         line(way, chunk, step, piece, place(chunk, block, piece), send, recv).wait_send()
 
-    def accumulate(matrix, chunks, block, vectors, kind):
-        columns = pl.ds(pl.multiple_of(block * rows, rows), rows)
+    def accumulate(matrix, chunks, block, vectors, kind, part_of=0, parts=1):
+        depth = rows // parts
+        columns = pl.ds(pl.multiple_of(block * rows + part_of * depth, depth), depth)
+        inside = pl.ds(part_of * depth, depth)
 
         @pl.loop(0, rows // tile)
         def _(i):
             part = pl.ds(pl.multiple_of(i * tile, tile), tile)
-            wide = jnp.concatenate([vectors[c, block] for c in chunks], axis=1)
+            wide = jnp.concatenate([vectors[c, block, inside] for c in chunks], axis=1)
             product = jnp.dot(matrix[part, columns], wide, preferred_element_type=jnp.float32)
             for n, c in enumerate(chunks):
                 one = product[:, n * width:(n + 1) * width]
@@ -126,17 +126,17 @@
     def rhs_place(chunk, block, piece):
         return rhs.at[chunk, block, pl.ds(piece * tall, tall)]
 
-    def rhs_pass(chunk, step):
-        pass_on(chunk, step, SOURCE_PIECES, rhs_place, rhs_send, rhs_recv)
-
-    def rhs_product(chunks, step):
+    def rhs_pass(chunk, step, pieces=range(SOURCE_PIECES)):
+        pass_on(chunk, step, pieces, rhs_place, rhs_send, rhs_recv)
+
+    def rhs_product(chunks, step, *quarter):
         if step == 0:
-            accumulate(inverse_v, chunks, panel, rhs, "set")
+            accumulate(inverse_v, chunks, panel, rhs, "set", *quarter)
         else:
             for _, block, exists, _ in ways(step):
                 @pl.when(exists)
                 def _(block=block):
-                    accumulate(inverse_v, chunks, block, rhs, "add")
+                    accumulate(inverse_v, chunks, block, rhs, "add", *quarter)
 
     def near_place(chunk, block, piece):
         return previous.at[chunk, block, pl.ds(piece * short, short)]
@@ -152,14 +152,18 @@
                         def _(way=way, piece=piece, here=here):
                             line(way, chunk, 0, piece, here, near_send, near_recv).start()
         else:
-            pass_on(chunk, step, NEAR[chunk], near_place, near_send, near_recv)
+            pass_on(chunk, step, range(NEAR[chunk]), near_place, near_send, near_recv)
 
     def previous_product(step):
+        parts = quarters if step == last and step > 0 else 1
+
         def one(block):
-            for chunk in range(CHUNKS):
-                for piece in range(NEAR[chunk], PIECES):
-                    to_zone(chunk, block, piece, near_place(chunk, block, piece)).wait_recv()
-            accumulate(coupling_v, (0, 1), block, previous, "subtract")
+            for part in range(parts):
+                for chunk in range(CHUNKS):
+                    for piece in range(part * PIECES // parts, (part + 1) * PIECES // parts):
+                        if piece >= NEAR[chunk]:
+                            to_zone(chunk, block, piece, near_place(chunk, block, piece)).wait_recv()
+                accumulate(coupling_v, (0, 1), block, previous, "subtract", part, parts)
 
         if step == 0:
             one(panel)
@@ -175,29 +179,33 @@
     def far_place(chunk, block, piece):
         return passing.at[block, pl.ds(piece * short, short)]
 
+    def source_sent():
+        for chunk in range(CHUNKS):
+            sent(chunk, SOURCE_PIECES, rhs_place, rhs_send, rhs_recv)
+
     def finish(chunk):
-        result = total[chunk].astype(mine.dtype)
-        out[0, :, columns_of(chunk)] = result
-
         @pl.when(has_next)
         def _():
-            mine[chunk] = result
+            mine[chunk] = total[chunk].astype(mine.dtype)
             near = NEAR[chunk]
-            for piece in range(near):
+            for piece in range(PIECES):
                 to_zone(chunk, panel, piece, own(chunk, piece)).start()
 
             def hand_over(block, piece):
-                from_ref = own(chunk, near + piece) if step == 0 else far_place(chunk, block, piece)
-                to_zone(chunk, block, near + piece, from_ref).start()
-
+                to_zone(chunk, block, near + piece, far_place(chunk, block, piece)).start()
+
+            if chunk == CHUNKS - 1:
+                source_sent()
             if near < PIECES:
                 for step in range(panels):
                     pass_on(
-                        chunk, step, PIECES - near, far_place, far_send, far_recv,
+                        chunk, step, range(PIECES - near), far_place, far_send, far_recv,
                         (lambda piece: own(chunk, near + piece)) if step == 0 else None, hand_over,
                     )
 
-    last = panels - 1
+        out[0, :, columns_of(chunk)] = total[chunk].astype(out.dtype)
+
+    last, quarters = panels - 1, min(4, rows // 128)
     is_first = jnp.logical_not(has_before)
 
     def in_first(action):
@@ -248,12 +256,20 @@
         @in_later
         def _():
             previous_pass(0, 0)
+        @in_first
+        def _():
+            rhs_product((1,), 0)
     else:
-        rhs_pass(1, last)
+        each = SOURCE_PIECES // quarters
+        for part in range(quarters):
+            rhs_pass(1, last, range(part * each, (part + 1) * each))
+
+            @in_first
+            def _(part=part):
+                rhs_product((1,), last, part, quarters)
 
     @in_first
     def _():
-        rhs_product((1,), last)
         load_coupling.wait()
 
     @in_later
@@ -278,9 +294,8 @@
 
     finish(1)
 
+    pl.when(jnp.logical_not(has_next))(source_sent)
     for chunk in range(CHUNKS):
-        sent(chunk, SOURCE_PIECES, rhs_place, rhs_send, rhs_recv)
-
         @pl.when(has_before)
         def _(chunk=chunk):
             sent(chunk, NEAR[chunk], near_place, near_send, near_recv)

time: 67 us -> 67.9 us (1.013)
  Pallas kernels: 65 us -> 65.9 us
    pallas_call x1, Pallas kernels: 65 us -> 65.9 us  [local(): pl.pallas_call(functools.partial(kernel, panels, zones), out_shape=jax.Sh...]
where the time goes in v4:
time: 67.9 us; the launch traced here: 67.7 us
  Pallas kernels  65.9 us (97%)
  local copies, waits for them, and re-layouts  1.84 us (3%)
    pallas_call x1, Pallas kernels, local(): pl.pallas_call(functools.partial(kernel, panels, zones), out_shape=jax.Sh...  65.9 us
    unnamed x3, local copies, waits for them, and re-layouts  1.84 us

profile of v4, /device:TPU:2, one launch (start us, length us, event | category | flops | bytes accessed | tf_op | source)
XLA Modules:
  0.0 67.7 jit_solution(8946567210791743839)
XLA Ops:
  0.0 0.0 copy-start
  0.0 1.0 %copy-done = bf16[1,1024,256]{2,1,0:T(8,128)(2,1)S(1)} copy-done((bf16[1,1024,256]{2,1,0:T(8,128)(2,1)S(1)}, bf16[1,1024,256]{2,1,0:T(8,128)(2,1)}, u32[]{:S(2)}) %copy-start) | copy-done | bytes 524312
  1.0 65.9 %shard_map.37 = bf16[1,1024,256]{2,1,0:T(8,128)(2,1)S(1)} custom-call(bf16[1,1024,256]{2,1,0:T(8,128)(2,1)S(1)} %copy-done, bf16[1,1024,4096]{2,1,0:T(8,128)(2,1)} %inverse.1, bf16[1,1024,4096]{2,1,0:T(8,128)(2,1)} %coupling.1), custom_call_target="tpu_custom_call" | custom-call | flops 4294967296 | bytes 16777216 | tf_op jit(solution)/shard_map/pallas_call | solution.py:323
  66.9 0.8 %copy.5 = bf16[1,1024,256]{2,1,0:T(8,128)(2,1)} copy(bf16[1,1024,256]{2,1,0:T(8,128)(2,1)S(1)} %shard_map.37) | data formatting | bytes 1048576
Async XLA Ops:
  0.0 1.0 %copy-start = (bf16[1,1024,256]{2,1,0:T(8,128)(2,1)S(1)}, bf16[1,1024,256]{2,1,0:T(8,128)(2,1)}, u32[]{:S(2)}) copy-start(bf16[1,1024,256]{2,1,0:T(8,128)(2,1)} %source.1) | copy-start | bytes 1572868

commit v5 on v4

--- a/solution.py
+++ b/solution.py
@@ -95,6 +95,8 @@
                             line(way, chunk, step, piece, here, send, recv, start).start()
                     if step > 0 and after is not None:
                         after(block, piece)
+            if step == 0 and after is not None:
+                after(panel, piece)
 
     def sent(chunk, pieces, place, send, recv):
         for step in range(panels - 1):
@@ -155,15 +157,11 @@
             pass_on(chunk, step, range(NEAR[chunk]), near_place, near_send, near_recv)
 
     def previous_product(step):
-        parts = quarters if step == last and step > 0 else 1
-
         def one(block):
-            for part in range(parts):
-                for chunk in range(CHUNKS):
-                    for piece in range(part * PIECES // parts, (part + 1) * PIECES // parts):
-                        if piece >= NEAR[chunk]:
-                            to_zone(chunk, block, piece, near_place(chunk, block, piece)).wait_recv()
-                accumulate(coupling_v, (0, 1), block, previous, "subtract", part, parts)
+            for chunk in range(CHUNKS):
+                for piece in range(NEAR[chunk], PIECES):
+                    to_zone(chunk, block, piece, near_place(chunk, block, piece)).wait_recv()
+            accumulate(coupling_v, (0, 1), block, previous, "subtract")
 
         if step == 0:
             one(panel)
@@ -179,23 +177,18 @@
     def far_place(chunk, block, piece):
         return passing.at[block, pl.ds(piece * short, short)]
 
-    def source_sent():
-        for chunk in range(CHUNKS):
-            sent(chunk, SOURCE_PIECES, rhs_place, rhs_send, rhs_recv)
-
     def finish(chunk):
         @pl.when(has_next)
         def _():
             mine[chunk] = total[chunk].astype(mine.dtype)
             near = NEAR[chunk]
-            for piece in range(PIECES):
+            for piece in range(near):
                 to_zone(chunk, panel, piece, own(chunk, piece)).start()
 
             def hand_over(block, piece):
-                to_zone(chunk, block, near + piece, far_place(chunk, block, piece)).start()
-
-            if chunk == CHUNKS - 1:
-                source_sent()
+                from_ref = own(chunk, near + piece) if step == 0 else far_place(chunk, block, piece)
+                to_zone(chunk, block, near + piece, from_ref).start()
+
             if near < PIECES:
                 for step in range(panels):
                     pass_on(
@@ -203,6 +196,7 @@
                         (lambda piece: own(chunk, near + piece)) if step == 0 else None, hand_over,
                     )
 
+    def give(chunk):
         out[0, :, columns_of(chunk)] = total[chunk].astype(out.dtype)
 
     last, quarters = panels - 1, min(4, rows // 128)
@@ -293,9 +287,12 @@
         finish(0)
 
     finish(1)
-
-    pl.when(jnp.logical_not(has_next))(source_sent)
     for chunk in range(CHUNKS):
+        give(chunk)
+
+    for chunk in range(CHUNKS):
+        sent(chunk, SOURCE_PIECES, rhs_place, rhs_send, rhs_recv)
+
         @pl.when(has_before)
         def _(chunk=chunk):
             sent(chunk, NEAR[chunk], near_place, near_send, near_recv)

time: 67.9 us -> 66.9 us (0.985)
  Pallas kernels: 65.9 us -> 64.9 us
    pallas_call x1, Pallas kernels: 65.9 us -> 64.9 us  [local(): pl.pallas_call(functools.partial(kernel, panels, zones), out_shape=jax.Sh...]
where the time goes in v5:
time: 66.9 us; the launch traced here: 66.8 us
  Pallas kernels  64.9 us (97%)
  local copies, waits for them, and re-layouts  1.84 us (3%)
    pallas_call x1, Pallas kernels, local(): pl.pallas_call(functools.partial(kernel, panels, zones), out_shape=jax.Sh...  64.9 us
    unnamed x3, local copies, waits for them, and re-layouts  1.84 us

profile of v5, /device:TPU:2, one launch (start us, length us, event | category | flops | bytes accessed | tf_op | source)
XLA Modules:
  0.0 66.8 jit_solution(549988056025479370)
XLA Ops:
  0.0 0.0 copy-start
  0.0 1.0 %copy-done = bf16[1,1024,256]{2,1,0:T(8,128)(2,1)S(1)} copy-done((bf16[1,1024,256]{2,1,0:T(8,128)(2,1)S(1)}, bf16[1,1024,256]{2,1,0:T(8,128)(2,1)}, u32[]{:S(2)}) %copy-start) | copy-done | bytes 524312
  1.0 64.9 %shard_map.37 = bf16[1,1024,256]{2,1,0:T(8,128)(2,1)S(1)} custom-call(bf16[1,1024,256]{2,1,0:T(8,128)(2,1)S(1)} %copy-done, bf16[1,1024,4096]{2,1,0:T(8,128)(2,1)} %inverse.1, bf16[1,1024,4096]{2,1,0:T(8,128)(2,1)} %coupling.1), custom_call_target="tpu_custom_call" | custom-call | flops 4294967296 | bytes 16777216 | tf_op jit(solution)/shard_map/pallas_call | solution.py:320
  66.0 0.8 %copy.5 = bf16[1,1024,256]{2,1,0:T(8,128)(2,1)} copy(bf16[1,1024,256]{2,1,0:T(8,128)(2,1)S(1)} %shard_map.37) | data formatting | bytes 1048576
Async XLA Ops:
  0.0 1.0 %copy-start = (bf16[1,1024,256]{2,1,0:T(8,128)(2,1)S(1)}, bf16[1,1024,256]{2,1,0:T(8,128)(2,1)}, u32[]{:S(2)}) copy-start(bf16[1,1024,256]{2,1,0:T(8,128)(2,1)} %source.1) | copy-start | bytes 1572868

commit v6 on v5

--- a/solution.py
+++ b/solution.py
@@ -24,7 +24,7 @@
     panel, zone = lax.axis_index("panel"), lax.axis_index("zone")
     _, rows, width = mine.shape
     tall, short = rows // SOURCE_PIECES, rows // PIECES
-    tile = min(rows, 512)
+    tile = min(rows, 1024)
     has_right, has_left = panel < panels - 1, panel > 0
     has_next, has_before = zone < zones - 1, zone > 0
 

time: 66.9 us -> 66.8 us (level)
  no operation moved by 1% of the time
where the time goes in v6:
time: 66.8 us; the launch traced here: 66.6 us
  Pallas kernels  64.8 us (97%)
  local copies, waits for them, and re-layouts  1.84 us (3%)
    pallas_call x1, Pallas kernels, local(): pl.pallas_call(functools.partial(kernel, panels, zones), out_shape=jax.Sh...  64.8 us
    unnamed x3, local copies, waits for them, and re-layouts  1.84 us

profile of v6, /device:TPU:2, one launch (start us, length us, event | category | flops | bytes accessed | tf_op | source)
XLA Modules:
  0.0 66.6 jit_solution(9526212588578841875)
XLA Ops:
  0.0 0.0 copy-start
  0.0 1.0 %copy-done = bf16[1,1024,256]{2,1,0:T(8,128)(2,1)S(1)} copy-done((bf16[1,1024,256]{2,1,0:T(8,128)(2,1)S(1)}, bf16[1,1024,256]{2,1,0:T(8,128)(2,1)}, u32[]{:S(2)}) %copy-start) | copy-done | bytes 524312
  1.0 64.8 %shard_map.37 = bf16[1,1024,256]{2,1,0:T(8,128)(2,1)S(1)} custom-call(bf16[1,1024,256]{2,1,0:T(8,128)(2,1)S(1)} %copy-done, bf16[1,1024,4096]{2,1,0:T(8,128)(2,1)} %inverse.1, bf16[1,1024,4096]{2,1,0:T(8,128)(2,1)} %coupling.1), custom_call_target="tpu_custom_call" | custom-call | flops 4294967296 | bytes 16777216 | tf_op jit(solution)/shard_map/pallas_call | solution.py:320
  65.8 0.8 %copy.5 = bf16[1,1024,256]{2,1,0:T(8,128)(2,1)} copy(bf16[1,1024,256]{2,1,0:T(8,128)(2,1)S(1)} %shard_map.37) | data formatting | bytes 1048576
Async XLA Ops:
  0.0 1.0 %copy-start = (bf16[1,1024,256]{2,1,0:T(8,128)(2,1)S(1)}, bf16[1,1024,256]{2,1,0:T(8,128)(2,1)}, u32[]{:S(2)}) copy-start(bf16[1,1024,256]{2,1,0:T(8,128)(2,1)} %source.1) | copy-start | bytes 1572868
